TPU v7x, 32 devices: a whole 2x2x4 slice. The times are simulated.
32 devices in a mesh: ia: 8 (over y, x, core), ja: 4 (over z).
Axes of the slice: x: 2, y: 2, z: 4, core: 2. Of those that a mesh axis runs over, the one named last changes fastest.
Arguments:
- amplitudes: bfloat16 [8, 8, 1600, 1600], P('ia', 'ja'), may hold values from -6 to 6
- df_slabs: bfloat16 [4, 128, 1600], P('ja'), may hold values from -0.359375 to 0.359375
- vir_irrep: int32 [25], replicated, may hold values from 0 to 1, as said below
- occ_irrep: int32 [8], replicated, may hold values from 0 to 1, as said below
- aux_irrep: int32 [4], P('ja'), may hold values from 0 to 1, as said below
Outputs:
- residual_window: float32 [8, 8, 128, 128], P('ia', 'ja')
Inputs may be any that keep to these rules, and one draw needn't show every extreme that they name: `vir_irrep`: both labels occur among the tiles. `occ_irrep`: both labels occur. `aux_irrep`: both labels occur.
All inputs are finite; a program needn't handle non-finite values.
Results may differ from a plain program's by a relative error of at most 0.0029.
Values may be sent and summed in bfloat16 or wider, within the bound.
No kernel may reach another device: no remote copies, remote signals or barrier semaphores. Data moves between devices by JAX's collectives and lax.ppermute only.
A program may use at most 64 MiB of HBM per device.

v0:
```python
import functools

import jax
import jax.numpy as jnp
from jax import lax
from jax.experimental import pallas as pl
from jax.experimental.pallas import tpu as pltpu
from jax.sharding import PartitionSpec as P

TILE = 64
ROWS = 16
SLOTS = 16
WIDTH = SLOTS * TILE
BLOCK = 256
BLOCKS = WIDTH // 128
GROUP = 4
F32 = jnp.float32
BF16 = jnp.bfloat16
VMEM_LIMIT = 32 * 1024 * 1024

smem = pl.BlockSpec(memory_space=pltpu.SMEM)
vmem = pl.BlockSpec(memory_space=pltpu.VMEM)
hbm = pl.BlockSpec(memory_space=pltpu.HBM)


def column_labels(vir_ref, tiles, columns):
    tile_of = lax.broadcasted_iota(jnp.int32, (1, columns), 1) // TILE
    labels = jnp.zeros((1, columns), jnp.int32)
    for tile in range(tiles):
        labels = jnp.where(tile_of == tile, vir_ref[tile], labels)
    return labels


def row_labels(vir_ref, first_row, rows, window):
    row = first_row + lax.broadcasted_iota(jnp.int32, (rows, 1), 0)
    labels = jnp.zeros((rows, 1), jnp.int32)
    for tile in range(window // TILE):
        labels = jnp.where(row // TILE == tile, vir_ref[tile], labels)
    return labels


def masked(block, rows_label, columns_label, aux):
    return jnp.where((rows_label ^ columns_label) == aux, block, jnp.zeros_like(block))


def piece_kernel(pieces, vir_hbm, aux_ref, slab_hbm, own_ref, piece_ref, vir_ref, slab_ref, sem):
    copies = [
        pltpu.make_async_copy(slab_hbm, slab_ref, sem.at[0]),
        pltpu.make_async_copy(vir_hbm, vir_ref, sem.at[1]),
    ]
    for copy in copies:
        copy.start()
    for copy in copies:
        copy.wait()
    count, columns, window = slab_ref.shape
    first = pl.multiple_of(lax.rem(lax.axis_index("ia"), pieces) * ROWS, ROWS)
    labels = column_labels(vir_ref, vir_ref.shape[0], columns)
    rows = row_labels(vir_ref, 0, window, window)
    for aux in range(count):
        own_ref[aux * window : (aux + 1) * window, :] = masked(slab_ref[aux].T, rows, labels, aux_ref[aux])
        piece_ref[aux * ROWS : (aux + 1) * ROWS, :] = own_ref[pl.ds(aux * window + first, ROWS), :]


def join_kernel(*refs):
    out_ref = refs[-1]
    at = 0
    for ref in refs[:-1]:
        out_ref[at : at + ref.shape[0], :] = ref[...]
        at += ref.shape[0]


def chunks(columns):
    step = 512
    starts = list(range(0, columns, step))
    if len(starts) > 1 and columns - starts[-1] < 128:
        starts.pop()
    return list(zip(starts, starts[1:] + [columns]))


def add_ladder(tile_ref, pair, slabs, ladder):
    columns = slabs.shape[1]
    window = ladder.shape[0]
    for lo, hi in chunks(columns):
        half = jnp.dot(slabs[...], tile_ref[0, pair, :, lo:hi], preferred_element_type=F32).astype(BF16)
        for start in range(0, slabs.shape[0], window):
            ladder = ladder + lax.dot_general(
                half[start : start + window],
                slabs[start : start + window, lo:hi],
                (((1,), (1,)), ((), ())),
                preferred_element_type=F32,
            )
    return ladder


def own_kernel(own_ref, t_ref, tile_ref, ladder_ref, sem):
    window = ladder_ref.shape[1]
    copies = []
    for pair in range(t_ref.shape[1]):
        copies.append(pltpu.make_async_copy(t_ref.at[0, pair], tile_ref.at[0, pair], sem.at[pair]))
        copies[-1].start()
    for pair in range(t_ref.shape[1]):
        copies[pair].wait()
        ladder_ref[pair] = add_ladder(tile_ref, pair, own_ref, jnp.zeros((window, window), F32))


def rest_kernel(pieces, others, vir_ref, occ_ref, ladder_ref, tile_ref, *refs):
    piece_refs = refs[:pieces]
    out_ref = refs[pieces]
    pairs = tile_ref.shape[1]
    send_ref = refs[pieces + 1]
    slabs = refs[-1]
    window = out_ref.shape[1]
    row = lax.axis_index("ia")
    column = lax.axis_index("ja") * pairs
    mine = lax.rem(row, pieces)
    for m in range(pieces):
        first = pl.multiple_of((mine ^ m) * ROWS, ROWS)
        for slab in range(others):
            slabs[pl.ds(slab * window + first, ROWS), :] = piece_refs[m][slab * ROWS : (slab + 1) * ROWS, :]
    left = row_labels(vir_ref, 0, window, window)
    right = column_labels(vir_ref, window // TILE, window)
    for pair in range(pairs):
        ladder = add_ladder(tile_ref, pair, slabs, ladder_ref[pair])
        keep = (left ^ right) == (occ_ref[row] ^ occ_ref[column + pair])
        out_ref[pair] = jnp.where(keep, ladder, jnp.zeros_like(ladder))
    for step in range(pairs):
        block = out_ref[lax.rem(row + step, pairs)]
        send_ref[step] = block.T.astype(BF16)


def places_of(vir_ref):
    places = []
    ones = jnp.int32(0)
    for tile in range(vir_ref.shape[0]):
        label = vir_ref[tile]
        places.append((label, jnp.where(label == 1, ones, tile - ones)))
        ones = ones + label
    return places, (vir_ref.shape[0] - ones, ones)


def tile_rows(place):
    return pl.ds(pl.multiple_of(place * TILE, TILE), TILE)


def compact_rows(slab, places, numbers, label, sorted_ref):
    tiles = len(places)
    for tile, (of, place) in enumerate(places):
        sorted_ref[of, tile_rows(place), :] = slab[tile * TILE : (tile + 1) * TILE, :]
    number = jnp.where(label == 1, numbers[1], numbers[0])
    block = sorted_ref[label, :WIDTH, :].T
    column = lax.broadcasted_iota(jnp.int32, (16, WIDTH), 1)
    mark = jnp.where((column == WIDTH - 1) & (number * 2 < tiles), 1.0, 0.0).astype(BF16)
    keep = column < number * TILE
    rows = block.shape[0]
    return jnp.concatenate(
        [jnp.where(keep, block[r : r + 16], mark) for r in range(0, rows, 16)], axis=0
    )


def compact_kernel(vir_hbm, aux_ref, slab_hbm, piece_ref, fits_ref, vir_ref, slab_ref, sorted_ref, turned_ref, sem):
    copies = [
        pltpu.make_async_copy(slab_hbm, slab_ref, sem.at[0]),
        pltpu.make_async_copy(vir_hbm, vir_ref, sem.at[1]),
    ]
    for copy in copies:
        copy.start()
    copies[1].wait()
    places, numbers = places_of(vir_ref)
    fits_ref[0] = jnp.where(jnp.maximum(numbers[0], numbers[1]) <= SLOTS, 1, 0)
    core = lax.rem(lax.axis_index("ia"), 2)
    copies[0].wait()
    for aux in range(slab_ref.shape[0]):
        label = aux_ref[aux] ^ vir_ref[core]
        turned_ref[...] = compact_rows(slab_ref[aux], places, numbers, label, sorted_ref)
        for q in range(BLOCKS):
            piece_ref[aux, q] = turned_ref[tile_rows(core), q * 128 : (q + 1) * 128]


def sort_kernel(
    vir_ref, occ_ref, aux_ref, after_ref, slab_hbm, t_hbm, own_ref, out_ref, stage_ref,
    slab_ref, rows_ref, lists_ref, slab_sem, sem,
):
    del after_ref
    pairs = t_hbm.shape[1]
    columns = t_hbm.shape[3]
    tiles = vir_ref.shape[0]
    row = lax.axis_index("ia")
    column = lax.axis_index("ja") * pairs
    full = columns // 128
    moves = [pltpu.make_async_copy(t_hbm.at[0, pair], stage_ref.at[pair], sem.at[pair]) for pair in range(pairs)]
    for move in moves:
        move.start()
    own_copy = pltpu.make_async_copy(slab_hbm, slab_ref, slab_sem)
    own_copy.start()
    places, numbers = places_of(vir_ref)
    for label in range(2):
        for place in range(SLOTS):
            lists_ref[label, place] = -1
    for tile, (label, place) in enumerate(places):
        lists_ref[label, place] = tile
    own_copy.wait()
    count, _, window = slab_ref.shape
    for aux in range(count):
        for chunk in range(2):
            label = aux_ref[aux] ^ vir_ref[chunk]
            block = compact_rows(slab_ref[aux], places, numbers, label, rows_ref)
            for q in range(BLOCKS):
                own_ref[aux, q, chunk * TILE : (chunk + 1) * TILE, :] = block[
                    chunk * TILE : (chunk + 1) * TILE, q * 128 : (q + 1) * 128
                ]
    lower = lax.broadcasted_iota(jnp.int32, (TILE, 128), 1) < TILE
    for pair in range(pairs):
        moves[pair].wait()
        symbol = occ_ref[row] ^ occ_ref[column + pair]

        for label in range(2):
            rows_of = jnp.where(label == 1, numbers[1], numbers[0])
            columns_of = jnp.where((label ^ symbol) == 1, numbers[1], numbers[0])

            def block(q, carry, label=label, rows_of=rows_of):
                known = [
                    jnp.clip(lists_ref[label ^ symbol, 2 * q + upper], 0, 2 * full - 1) for upper in range(2)
                ]
                spots = [pl.ds(pl.multiple_of((k // 2) * 128, 128), 128) for k in known]
                sides = [lax.rem(k, 2) for k in known]

                def move(left, right, number):
                    for group in range(0, number, GROUP):
                        joined = []
                        for place in range(group, group + GROUP):
                            rows = tile_rows(jnp.maximum(lists_ref[label, place], 0))
                            low, high = [stage_ref[pair, rows, spot] for spot in spots]
                            if left and not right:
                                value = pltpu.roll(jnp.where(lower, high, low), TILE, 1)
                            else:
                                value = jnp.where(
                                    lower,
                                    pltpu.roll(low, TILE, 1) if left else low,
                                    high if right else pltpu.roll(high, TILE, 1),
                                )
                            joined.append(value)
                        out_ref[2 * pair + label, q, group * TILE : (group + GROUP) * TILE, :] = (
                            jnp.concatenate(joined, axis=0)
                        )

                for left in range(2):
                    for right in range(2):
                        here = (sides[0] == left) & (sides[1] == right)
                        few = rows_of <= SLOTS - GROUP
                        pl.when(here & few)(functools.partial(move, left, right, SLOTS - GROUP))
                        pl.when(here & jnp.logical_not(few))(functools.partial(move, left, right, SLOTS))
                return carry

            lax.fori_loop(0, jnp.minimum((columns_of + 1) // 2, BLOCKS), block, 0)
        empty = jnp.zeros((TILE, TILE), BF16)
        if columns % 128:
            last = vir_ref[tiles - 1]
            end = jnp.where(last == 1, numbers[1], numbers[0]) - 1
            label = last ^ symbol
            q = jnp.minimum(end // 2, BLOCKS - 1)
            for upper in range(2):

                @pl.when((lax.rem(end, 2) == upper) & (end < SLOTS))
                def _(upper=upper):
                    for place in range(SLOTS):
                        rows = tile_rows(jnp.maximum(lists_ref[label, place], 0))
                        value = stage_ref[pair, rows, full * 128 :]
                        at = (2 * pair + label, q, slice(place * TILE, (place + 1) * TILE), slice(None))
                        both = [value, empty] if upper == 0 else [out_ref[at][:, :TILE], value]
                        out_ref[at] = jnp.concatenate(both, axis=1)

        for label in range(2):
            number = jnp.where((label ^ symbol) == 1, numbers[1], numbers[0])

            def clear_block(q, carry):
                out_ref[2 * pair + label, q] = jnp.zeros((WIDTH, 128), BF16)
                return carry

            lax.fori_loop((number + 1) // 2, BLOCKS, clear_block, 0)

            @pl.when((lax.rem(number, 2) == 1) & (number < SLOTS))
            def _():
                q = number // 2
                for place in range(SLOTS):
                    rows = slice(place * TILE, (place + 1) * TILE)
                    value = out_ref[2 * pair + label, q, rows, :]
                    out_ref[2 * pair + label, q, rows, :] = jnp.concatenate([value[:, :TILE], empty], axis=1)

        for label in range(2):

            def clear(place, carry):
                for q in range(BLOCKS):
                    out_ref[2 * pair + label, q, tile_rows(place), :] = jnp.zeros((TILE, 128), BF16)
                return carry

            lax.fori_loop(numbers[label], SLOTS, clear, 0)


def product_kernel(arrived, vir_ref, occ_ref, aux_ref, own_ref, sorted_ref, stage_ref, *refs):
    del stage_ref
    mine_refs, their_refs = refs[:arrived], refs[arrived : 2 * arrived]
    out_ref = refs[2 * arrived]
    pairs, window, _ = out_ref.shape
    send_ref = refs[2 * arrived + 1]
    slabs_ref, half_ref, place_ref = refs[-3:]
    count = own_ref.shape[0]
    total = count * (arrived + 1)
    tiles = vir_ref.shape[0]
    row = lax.axis_index("ia")
    column = lax.axis_index("ja") * pairs
    core = lax.rem(row, 2)
    ones = jnp.int32(0)
    for tile in range(tiles):
        ones = ones + vir_ref[tile]
    smaller = jnp.where(ones * 2 < tiles, 1, 0)

    auxes = [aux_ref[aux] for aux in range(count)]
    for ref in mine_refs:
        for aux in range(count):
            mark = ref[aux, BLOCKS - 1, :16, :].astype(F32)
            marked = jnp.max(mark) > 0.5
            label = jnp.where(marked, smaller, 1 - smaller)
            auxes.append(label ^ vir_ref[core])
    places = [[jnp.int32(0)] * 2 for _ in range(total)]
    rows_of = [jnp.int32(0), jnp.int32(0)]
    labels = [[aux ^ vir_ref[chunk] for chunk in range(2)] for aux in auxes]
    for slab in range(total):
        for chunk in range(2):
            label = labels[slab][chunk]
            places[slab][chunk] = jnp.where(label == 1, rows_of[1], rows_of[0])
            rows_of = [rows_of[0] + (1 - label) * TILE, rows_of[1] + label * TILE]
    first_blocks = (rows_of[0] + (BLOCK - 1)) // BLOCK
    blocks = first_blocks + (rows_of[1] + (BLOCK - 1)) // BLOCK
    for slab in range(total):
        for chunk in range(2):
            place_ref[slab, chunk] = places[slab][chunk] + labels[slab][chunk] * first_blocks * BLOCK

    def at(slab, chunk):
        return pl.ds(pl.multiple_of(place_ref[slab, chunk], TILE), TILE)

    for aux in range(count):
        for chunk in range(2):
            for q in range(BLOCKS):
                slabs_ref[at(aux, chunk), q * 128 : (q + 1) * 128] = own_ref[
                    aux, q, chunk * TILE : (chunk + 1) * TILE, :
                ]
    for m in range(arrived):
        for aux in range(count):
            slab = (m + 1) * count + aux
            for q in range(BLOCKS):
                slabs_ref[at(slab, core), q * 128 : (q + 1) * 128] = mine_refs[m][aux, q]
                slabs_ref[at(slab, 1 - core), q * 128 : (q + 1) * 128] = their_refs[m][aux, q]

    left = row_labels(vir_ref, 0, window, window)
    right = column_labels(vir_ref, window // TILE, window)

    def one_pair(pair, carry):
        symbol = occ_ref[row] ^ occ_ref[column + pair]
        out_ref[pair] = jnp.zeros((window, window), F32)

        @pl.when((vir_ref[0] != vir_ref[1]) | (symbol == 0))
        def _():
            def first(block, inner):
                label = jnp.where(block < first_blocks, 0, 1)
                rows = pl.ds(pl.multiple_of(block * BLOCK, BLOCK), BLOCK)
                for lo in range(0, WIDTH, 512):
                    half_ref[rows, lo : lo + 512] = jnp.dot(
                        slabs_ref[rows, :],
                        jnp.concatenate(
                            [sorted_ref[2 * pair + label, (lo + at) // 128] for at in range(0, 512, 128)], axis=1
                        ),
                        preferred_element_type=F32,
                    ).astype(BF16)
                return inner

            lax.fori_loop(0, blocks, first, 0)
            ladder = jnp.zeros((window, window), F32)
            for slab in range(total):
                halves = jnp.concatenate([half_ref[at(slab, 0), :], half_ref[at(slab, 1), :]], axis=0)
                others = jnp.concatenate([slabs_ref[at(slab, 0), :], slabs_ref[at(slab, 1), :]], axis=0)
                ladder = ladder + lax.dot_general(
                    halves, others, (((1,), (1,)), ((), ())), preferred_element_type=F32
                )
            out_ref[pair] = jnp.where((left ^ right) == symbol, ladder, jnp.zeros_like(ladder))

        return carry

    lax.fori_loop(0, pairs, one_pair, 0)
    for step in range(pairs):
        block = out_ref[lax.rem(row + step, pairs)]
        send_ref[step] = block.T.astype(BF16)


def add_kernel(ladder_ref, *refs):
    out_ref = refs[-1]
    pairs = ladder_ref.shape[0]
    row = lax.axis_index("ia")
    for step in range(pairs):
        slot = lax.rem(row + (pairs - step), pairs)
        block = refs[step][min(step, refs[step].shape[0] - 1)]
        out_ref[0, slot] = ladder_ref[slot] + block.astype(F32)


def in_hbm(array):
    return pltpu.with_memory_space_constraint(array, pltpu.HBM)


def params(**kwargs):
    return pltpu.CompilerParams(vmem_limit_bytes=VMEM_LIMIT, **kwargs)


def solution(mesh):
    rows_of_mesh = mesh.shape["ia"]
    columns_of_mesh = mesh.shape["ja"]

    def general(amplitudes, df_slabs, vir_irrep, occ_irrep, aux_irrep):
        occ_rows, pairs, vir_count, _ = amplitudes.shape
        count, window, _ = df_slabs.shape
        assert occ_rows == 1 and rows_of_mesh == pairs * columns_of_mesh
        pieces = 1
        while pieces * 2 <= min(rows_of_mesh, window // ROWS):
            pieces *= 2
        assert pieces * ROWS == window and rows_of_mesh % pieces == 0
        others = (columns_of_mesh - 1) * count

        own, piece = pl.pallas_call(
            functools.partial(piece_kernel, pieces),
            out_shape=(
                jax.ShapeDtypeStruct((count * window, vir_count), BF16),
                jax.ShapeDtypeStruct((count * ROWS, vir_count), BF16),
            ),
            in_specs=[hbm, smem, hbm],
            out_specs=(vmem, vmem),
            scratch_shapes=[
                pltpu.SMEM(vir_irrep.shape, jnp.int32),
                pltpu.VMEM((count, vir_count, window), BF16),
                pltpu.SemaphoreType.DMA((2,)),
            ],
            compiler_params=params(),
            name="mask_slab",
        )(in_hbm(vir_irrep), aux_irrep, in_hbm(jnp.transpose(df_slabs, (0, 2, 1))))
        got = [
            lax.ppermute(piece, "ja", [(j, j ^ s) for j in range(columns_of_mesh)])
            for s in range(columns_of_mesh - 1, 0, -1)
        ]
        tile, ladder = pl.pallas_call(
            own_kernel,
            out_shape=(
                pltpu.VMEM(amplitudes.shape, BF16),
                jax.ShapeDtypeStruct((pairs, window, window), F32),
            ),
            in_specs=[vmem, hbm],
            out_specs=(vmem, vmem),
            scratch_shapes=[pltpu.SemaphoreType.DMA((pairs,))],
            compiler_params=params(),
            cost_estimate=pl.CostEstimate(
                flops=2 * pairs * count * window * vir_count * vir_count,
                bytes_accessed=pairs * vir_count * vir_count * 2,
                transcendentals=0,
            ),
            name="own_slab",
        )(own, in_hbm(amplitudes))
        got, ladder = lax.optimization_barrier((got, ladder))
        joined = pl.pallas_call(
            join_kernel,
            out_shape=jax.ShapeDtypeStruct((others * ROWS, vir_count), BF16),
            in_specs=[vmem] * len(got),
            out_specs=vmem,
            compiler_params=params(),
            name="join_pieces",
        )(*got)
        held = {0: joined}
        for m in range(2, pieces, 2):
            held[m] = lax.ppermute(joined, "ia", [(i, i ^ m) for i in range(rows_of_mesh)])
        for m in range(0, pieces, 2):
            held[m + 1] = lax.ppermute(held[m], "ia", [(i, i ^ 1) for i in range(rows_of_mesh)])

        out = pl.pallas_call(
            functools.partial(rest_kernel, pieces, others),
            out_shape=(
                jax.ShapeDtypeStruct((pairs, window, window), F32),
                jax.ShapeDtypeStruct((pairs, window, window), BF16),
            ),
            in_specs=[smem, smem, vmem, vmem] + [vmem] * pieces,
            out_specs=(vmem, vmem),
            scratch_shapes=[pltpu.VMEM((others * window, vir_count), BF16)],
            compiler_params=params(),
            cost_estimate=pl.CostEstimate(
                flops=2 * pairs * others * window * vir_count * vir_count,
                bytes_accessed=others * window * vir_count * 2,
                transcendentals=0,
            ),
            name="other_slabs",
        )(vir_irrep, occ_irrep, ladder, pltpu.with_memory_space_constraint(tile, pltpu.VMEM), *[held[m] for m in range(pieces)])
        return tuple(out)

    def first_piece(df_slabs, vir_irrep, aux_irrep):
        count, window, vir_count = df_slabs.shape
        return pl.pallas_call(
            compact_kernel,
            out_shape=(
                jax.ShapeDtypeStruct((count, BLOCKS, TILE, 128), BF16),
                jax.ShapeDtypeStruct((1,), jnp.int32),
            ),
            in_specs=[hbm, smem, hbm],
            out_specs=(vmem, smem),
            scratch_shapes=[
                pltpu.SMEM(vir_irrep.shape, jnp.int32),
                pltpu.VMEM((count, vir_count, window), BF16),
                pltpu.VMEM((2, vir_count, window), BF16),
                pltpu.VMEM((window, WIDTH), BF16),
                pltpu.SemaphoreType.DMA((2,)),
            ],
            compiler_params=params(),
            name="compact_piece",
        )(in_hbm(vir_irrep), aux_irrep, in_hbm(jnp.transpose(df_slabs, (0, 2, 1))))

    def start_compact(piece, amplitudes, df_slabs, vir_irrep, occ_irrep, aux_irrep):
        _, pairs, vir_count, _ = amplitudes.shape
        count, window, _ = df_slabs.shape
        tiles = vir_irrep.shape[0]
        slab = in_hbm(jnp.transpose(df_slabs, (0, 2, 1)))
        mine = [
            lax.ppermute(piece, "ja", [(j, j ^ s) for j in range(columns_of_mesh)])
            for s in range(columns_of_mesh - 1, 0, -1)
        ]
        own, tile, stage = pl.pallas_call(
            sort_kernel,
            out_shape=(
                jax.ShapeDtypeStruct((count, BLOCKS, window, 128), BF16),
                pltpu.VMEM((2 * pairs, BLOCKS, WIDTH, 128), BF16),
                pltpu.VMEM((pairs, vir_count, vir_count), BF16),
            ),
            in_specs=[smem, smem, smem, pl.BlockSpec(memory_space=pl.ANY), hbm, hbm],
            out_specs=(vmem, vmem, vmem),
            scratch_shapes=[
                pltpu.VMEM((count, vir_count, window), BF16),
                pltpu.VMEM((2, vir_count, window), BF16),
                pltpu.SMEM((2, tiles), jnp.int32),
                pltpu.SemaphoreType.DMA,
                pltpu.SemaphoreType.DMA((pairs,)),
            ],
            compiler_params=params(),
            cost_estimate=pl.CostEstimate(
                flops=pairs * 2 * WIDTH * WIDTH * 8,
                bytes_accessed=pairs * vir_count * vir_count * 2,
                transcendentals=0,
            ),
            name="sort_amplitudes",
        )(vir_irrep, occ_irrep, aux_irrep, piece, slab, in_hbm(amplitudes))
        return mine, own, tile, stage

    def end_compact(mine, own, tile, stage, amplitudes, df_slabs, vir_irrep, occ_irrep, aux_irrep):
        _, pairs, _, _ = amplitudes.shape
        count, window, _ = df_slabs.shape
        total = count * columns_of_mesh
        rows = (total * window // BLOCK + 1) * BLOCK
        theirs = [lax.ppermute(p, "ia", [(i, i ^ 1) for i in range(rows_of_mesh)]) for p in mine]
        return pl.pallas_call(
            functools.partial(product_kernel, len(mine)),
            out_shape=(
                jax.ShapeDtypeStruct((pairs, window, window), F32),
                jax.ShapeDtypeStruct((pairs, window, window), BF16),
            ),
            in_specs=[smem, smem, smem, vmem, vmem, pl.BlockSpec(memory_space=pl.ANY)] + [vmem] * (2 * len(mine)),
            out_specs=(vmem, vmem),
            scratch_shapes=[
                pltpu.VMEM((rows, WIDTH), BF16),
                pltpu.VMEM((rows, WIDTH), BF16),
                pltpu.SMEM((total, 2), jnp.int32),
            ],
            compiler_params=params(),
            cost_estimate=pl.CostEstimate(
                flops=2 * pairs * total * window * WIDTH * WIDTH,
                bytes_accessed=total * window * WIDTH * 2,
                transcendentals=0,
            ),
            name="products",
        )(
            vir_irrep, occ_irrep, aux_irrep, own,
            pltpu.with_memory_space_constraint(tile, pltpu.VMEM),
            pltpu.with_memory_space_constraint(stage, pltpu.VMEM),
            *mine, *theirs,
        )

    def finish(ladder, sends):
        pairs = ladder.shape[0]

        def moves(step):
            return [
                (
                    i * columns_of_mesh + j,
                    (j * pairs + (i + step) % pairs) * columns_of_mesh + i // pairs,
                )
                for i in range(rows_of_mesh)
                for j in range(columns_of_mesh)
            ]

        if pairs != 2:
            return ladder, [
                lax.ppermute(sends[step : step + 1], ("ia", "ja"), moves(step)) for step in range(pairs)
            ]
        first = lax.ppermute(sends, ("ia", "ja"), moves(0))
        second = lax.ppermute(first, "ia", [(i, i ^ 1) for i in range(rows_of_mesh)])
        return ladder, [first, second]

    def add(ladder, received):
        pairs, window, _ = ladder.shape
        return pl.pallas_call(
            add_kernel,
            out_shape=jax.ShapeDtypeStruct((1, pairs, window, window), F32),
            in_specs=[vmem] * (pairs + 1),
            out_specs=vmem,
            compiler_params=params(),
            name="add_transposed",
        )(ladder, *received)

    def local(amplitudes, df_slabs, vir_irrep, occ_irrep, aux_irrep):
        window = df_slabs.shape[1]
        operands = (amplitudes, df_slabs, vir_irrep, occ_irrep, aux_irrep)
        if window != 2 * TILE or rows_of_mesh % 2:
            return add(*finish(*general(*operands)))
        piece, fits = first_piece(df_slabs, vir_irrep, aux_irrep)

        def compact():
            mine, own, tile, stage = start_compact(piece, *operands)
            mine, own = lax.optimization_barrier((mine, own))
            return add(*finish(*end_compact(mine, own, tile, stage, *operands)))

        return lax.cond(fits[0] == 1, compact, lambda: add(*finish(*general(*operands))))

    return jax.shard_map(
        local,
        mesh=mesh,
        in_specs=(P("ia", "ja", None, None), P("ja", None, None), P(), P(), P("ja")),
        out_specs=P("ia", "ja", None, None),
        check_vma=False,
    )
```

profile of v0, /device:TPU:7, one launch (start us, length us, event | category | flops | bytes accessed | tf_op | source)
XLA Modules:
  0.0 39.5 jit_solution(12316209762105147895)
XLA Ops:
  0.7 1.6 %compact_piece.1 = (bf16[1,8,64,128]{3,2,1,0:T(8,128)(2,1)S(1)}, s32[1]{0:T(128)}) custom-call(s32[25]{0:T(128)} %vir_hbm.1, s32[1]{0:T(128)S(6)} %copy.10.aux_ref, bf16[1,1600,128]{2,1,0:T(8,128)(2,1)} %bitcast.4), custom_call_target="tpu_custom_call" | custom-call | tf_op jit(solution)/shard_map/compact_piece/pallas_call | solution.py:499
  2.9 35.9 %conditional.1 = (f32[1,2,128,128]{3,2,1,0:T(8,128)S(1)}) conditional(s32[]{:T(128)} %bitcast.3, (bf16[1,128,1600]{1,2,0:T(8,128)(2,1)}, s32[25]{0:T(128)}, s32[1]{0:T(128)}, bf16[1,2,1600,1600]{3,2,1,0:T(8,128)(2,1)}, s32[8]{0:T(128)}) %tuple.13, (bf16[1,8,64,128]{3,2,1,0:T(8,128)(2,1)S(1)}, bf16[1,128,1600]{1,2,0:T(8,128)(2,1)}, s32[25]{0:T(128)}, ...), branch_computations={%region_0.0_spmd, %region_1.0_spmd} | conditional | flops 5242880000 | bytes 16909360 | solution.py:630
  2.9 0.0 copy-start.2
  2.9 0.0 copy-start.4
  2.9 1.4 %collective-permute-start.14 = (bf16[1,8,64,128]{3,2,1,0:T(8,128)(2,1)S(1)}, bf16[1,8,64,128]{3,2,1,0:T(8,128)(2,1)S(1)}, u32[]{:S(2)}, u32[]{:S(2)}) collective-permute-start(bf16[1,8,64,128]{3,2,1,0:T(8,128)(2,1)S(1)} %get-tuple-element.48.after_ref), channel_id=1, source_target_pairs={{0,1},{1,0},{2,3},{3,2},{4,5},{5,4},{6,7},{7,6},{8,9},{9,8},{10,11... | collective-permute-start | bytes 393224 | tf_op jit(solution)/shard_map/cond/branch_1_fun/ppermute | solution.py:524
  4.3 2.3 %collective-permute-start.13 = (bf16[1,8,64,128]{3,2,1,0:T(8,128)(2,1)S(1)}, bf16[1,8,64,128]{3,2,1,0:T(8,128)(2,1)S(1)}, u32[]{:S(2)}, u32[]{:S(2)}) collective-permute-start(bf16[1,8,64,128]{3,2,1,0:T(8,128)(2,1)S(1)} %get-tuple-element.48.after_ref), channel_id=1, source_target_pairs={{0,2},{1,3},{2,0},{3,1},{4,6},{5,7},{6,4},{7,5},{8,10},{9,11},{10,... | collective-permute-start | bytes 393224 | tf_op jit(solution)/shard_map/cond/branch_1_fun/ppermute | solution.py:524
  6.6 0.0 collective-permute-start.12
  6.6 12.1 %sort_amplitudes.1 = (bf16[1,8,128,128]{3,2,1,0:T(8,128)(2,1)S(1)}, bf16[4,8,1024,128]{3,2,1,0:T(8,128)(2,1)S(1)}, bf16[2,1600,1600]{2,1,0:T(8,128)(2,1)S(1)}) custom-call(s32[25]{0:T(128)} %get-tuple-element.45.vir_ref, s32[8]{0:T(128)} %get-tuple-element.46.occ_ref, s32[1]{0:T(128)} %get-tuple-element.47.aux_ref, ...), custom_call_target="tpu_custom_call" | custom-call | flops 33554432 | bytes 10240000 | tf_op jit(solution)/shard_map/cond/branch_1_fun/sort_amplitudes/pallas_call | solution.py:527
  18.7 0.0 collective-permute-done.14.refs_2_
  18.8 0.0 collective-permute-done.13.refs_1_
  18.8 0.0 collective-permute-done.12.refs_0_
  18.8 1.5 %collective-permute-start.15 = (bf16[1,8,64,128]{3,2,1,0:T(8,128)(2,1)S(1)}, bf16[1,8,64,128]{3,2,1,0:T(8,128)(2,1)S(1)}, u32[]{:S(2)}, u32[]{:S(2)}) collective-permute-start(bf16[1,8,64,128]{3,2,1,0:T(8,128)(2,1)S(1)} %collective-permute-done.12.refs_0_), channel_id=1, source_target_pairs={{0,4},{4,0},{8,12},{12,8},{16,20},{20,16},{24,28},{28,24},{1,5},{5... | collective-permute-start | bytes 393224 | tf_op jit(solution)/shard_map/cond/branch_1_fun/ppermute | solution.py:558
  20.3 0.1 collective-permute-start.16
  20.3 0.4 %collective-permute-start.17 = (bf16[1,8,64,128]{3,2,1,0:T(8,128)(2,1)S(1)}, bf16[1,8,64,128]{3,2,1,0:T(8,128)(2,1)S(1)}, u32[]{:S(2)}, u32[]{:S(2)}) collective-permute-start(bf16[1,8,64,128]{3,2,1,0:T(8,128)(2,1)S(1)} %collective-permute-done.14.refs_2_), channel_id=1, source_target_pairs={{0,4},{4,0},{8,12},{12,8},{16,20},{20,16},{24,28},{28,24},{1,5},{5... | collective-permute-start | bytes 393224 | tf_op jit(solution)/shard_map/cond/branch_1_fun/ppermute | solution.py:558
  20.8 0.5 %collective-permute-done.15.refs_3_ = bf16[1,8,64,128]{3,2,1,0:T(8,128)(2,1)S(1)} collective-permute-done((bf16[1,8,64,128]{3,2,1,0:T(8,128)(2,1)S(1)}, bf16[1,8,64,128]{3,2,1,0:T(8,128)(2,1)S(1)}, u32[]{:S(2)}, u32[]{:S(2)}) %collective-permute-start.15) | collective-permute-done | bytes 131104 | tf_op jit(solution)/shard_map/cond/branch_1_fun/ppermute | solution.py:558
  21.2 0.4 collective-permute-done.16.refs_4_
  21.6 0.2 collective-permute-done.17.refs_5_
  21.8 0.0 copy-done.2
  21.8 0.0 copy-done.4
  21.8 6.9 %products.1 = (f32[2,128,128]{2,1,0:T(8,128)S(1)}, bf16[2,128,128]{2,1,0:T(8,128)(2,1)S(1)}) custom-call(s32[25]{0:T(128)S(1)} %copy-done.2, s32[8]{0:T(128)S(1)} %copy-done.4, s32[1]{0:T(128)} %get-tuple-element.47.aux_ref, bf16[1,8,128,128]{3,2,1,0:T(8,128)(2,1)S(1)} %get-tuple-element.52.own_ref, ...), custom_call_target="tpu_custom_call" | custom-call | flops 2147483648 | bytes 1048576 | tf_op jit(solution)/shard_map/cond/branch_1_fun/products/pallas_call | solution.py:559
  28.7 2.6 %collective-permute-start.18 = (bf16[2,128,128]{2,1,0:T(8,128)(2,1)S(1)}, bf16[2,128,128]{2,1,0:T(8,128)(2,1)S(1)}, u32[]{:S(2)}, u32[]{:S(2)}) collective-permute-start(bf16[2,128,128]{2,1,0:T(8,128)(2,1)S(1)} %get-tuple-element.59), channel_id=1, source_target_pairs={{0,0},{1,8},{2,16},{3,24},{4,4},{5,12},{6,20},{7,28},{8,1},{9,9},{... | collective-permute-start | bytes 196616 | tf_op jit(solution)/shard_map/cond/branch_1_fun/ppermute | solution.py:603
  31.3 6.0 %collective-permute-done.18.refs_0_ = bf16[2,128,128]{2,1,0:T(8,128)(2,1)S(1)} collective-permute-done((bf16[2,128,128]{2,1,0:T(8,128)(2,1)S(1)}, bf16[2,128,128]{2,1,0:T(8,128)(2,1)S(1)}, u32[]{:S(2)}, u32[]{:S(2)}) %collective-permute-start.18) | collective-permute-done | bytes 65568 | tf_op jit(solution)/shard_map/cond/branch_1_fun/ppermute | solution.py:603
  37.3 0.0 collective-permute-start.19
  37.3 1.3 %collective-permute-done.19.refs_1_ = bf16[2,128,128]{2,1,0:T(8,128)(2,1)S(1)} collective-permute-done((bf16[2,128,128]{2,1,0:T(8,128)(2,1)S(1)}, bf16[2,128,128]{2,1,0:T(8,128)(2,1)S(1)}, u32[]{:S(2)}, u32[]{:S(2)}) %collective-permute-start.19) | collective-permute-done | bytes 65568 | tf_op jit(solution)/shard_map/cond/branch_1_fun/ppermute | solution.py:604
  38.8 0.0 copy-start
  38.8 0.6 %copy-done = f32[1,2,128,128]{3,2,1,0:T(8,128)} copy-done((f32[1,2,128,128]{3,2,1,0:T(8,128)}, f32[1,2,128,128]{3,2,1,0:T(8,128)S(1)}, u32[]{:S(2)}) %copy-start) | copy-done | bytes 131096
  (1 shorter events, 0.0 us)
Async XLA Ops:
  2.9 18.9 %copy-start.2 = (s32[25]{0:T(128)S(1)}, s32[25]{0:T(128)}, u32[]{:S(2)}) copy-start(s32[25]{0:T(128)} %get-tuple-element.45.vir_ref) | copy-start | bytes 304 | tf_op jit(solution)/shard_map/cond
  2.9 18.9 %copy-start.4 = (s32[8]{0:T(128)S(1)}, s32[8]{0:T(128)}, u32[]{:S(2)}) copy-start(s32[8]{0:T(128)} %get-tuple-element.46.occ_ref) | copy-start | bytes 100 | tf_op jit(solution)/shard_map/cond
  2.9 15.8 %collective-permute-start.14 = (bf16[1,8,64,128]{3,2,1,0:T(8,128)(2,1)S(1)}, bf16[1,8,64,128]{3,2,1,0:T(8,128)(2,1)S(1)}, u32[]{:S(2)}, u32[]{:S(2)}) collective-permute-start(bf16[1,8,64,128]{3,2,1,0:T(8,128)(2,1)S(1)} %get-tuple-element.48.after_ref), channel_id=1, source_target_pairs={{0,1},{1,0},{2,3},{3,2},{4,5},{5,4},{6,7},{7,6},{8,9},{9,8},{10,11... | collective-permute-start | bytes 393224 | tf_op jit(solution)/shard_map/cond/branch_1_fun/ppermute | solution.py:524
  4.3 14.5 %collective-permute-start.13 = (bf16[1,8,64,128]{3,2,1,0:T(8,128)(2,1)S(1)}, bf16[1,8,64,128]{3,2,1,0:T(8,128)(2,1)S(1)}, u32[]{:S(2)}, u32[]{:S(2)}) collective-permute-start(bf16[1,8,64,128]{3,2,1,0:T(8,128)(2,1)S(1)} %get-tuple-element.48.after_ref), channel_id=1, source_target_pairs={{0,2},{1,3},{2,0},{3,1},{4,6},{5,7},{6,4},{7,5},{8,10},{9,11},{10,... | collective-permute-start | bytes 393224 | tf_op jit(solution)/shard_map/cond/branch_1_fun/ppermute | solution.py:524
  6.6 12.2 %collective-permute-start.12 = (bf16[1,8,64,128]{3,2,1,0:T(8,128)(2,1)S(1)}, bf16[1,8,64,128]{3,2,1,0:T(8,128)(2,1)S(1)}, u32[]{:S(2)}, u32[]{:S(2)}) collective-permute-start(bf16[1,8,64,128]{3,2,1,0:T(8,128)(2,1)S(1)} %get-tuple-element.48.after_ref), channel_id=1, source_target_pairs={{0,3},{1,2},{2,1},{3,0},{4,7},{5,6},{6,5},{7,4},{8,11},{9,10},{10,... | collective-permute-start | bytes 393224 | tf_op jit(solution)/shard_map/cond/branch_1_fun/ppermute | solution.py:524
  18.8 2.5 %collective-permute-start.15 = (bf16[1,8,64,128]{3,2,1,0:T(8,128)(2,1)S(1)}, bf16[1,8,64,128]{3,2,1,0:T(8,128)(2,1)S(1)}, u32[]{:S(2)}, u32[]{:S(2)}) collective-permute-start(bf16[1,8,64,128]{3,2,1,0:T(8,128)(2,1)S(1)} %collective-permute-done.12.refs_0_), channel_id=1, source_target_pairs={{0,4},{4,0},{8,12},{12,8},{16,20},{20,16},{24,28},{28,24},{1,5},{5... | collective-permute-start | bytes 393224 | tf_op jit(solution)/shard_map/cond/branch_1_fun/ppermute | solution.py:558
  20.3 1.3 %collective-permute-start.16 = (bf16[1,8,64,128]{3,2,1,0:T(8,128)(2,1)S(1)}, bf16[1,8,64,128]{3,2,1,0:T(8,128)(2,1)S(1)}, u32[]{:S(2)}, u32[]{:S(2)}) collective-permute-start(bf16[1,8,64,128]{3,2,1,0:T(8,128)(2,1)S(1)} %collective-permute-done.13.refs_1_), channel_id=1, source_target_pairs={{0,4},{4,0},{8,12},{12,8},{16,20},{20,16},{24,28},{28,24},{1,5},{5... | collective-permute-start | bytes 393224 | tf_op jit(solution)/shard_map/cond/branch_1_fun/ppermute | solution.py:558
  20.3 1.5 %collective-permute-start.17 = (bf16[1,8,64,128]{3,2,1,0:T(8,128)(2,1)S(1)}, bf16[1,8,64,128]{3,2,1,0:T(8,128)(2,1)S(1)}, u32[]{:S(2)}, u32[]{:S(2)}) collective-permute-start(bf16[1,8,64,128]{3,2,1,0:T(8,128)(2,1)S(1)} %collective-permute-done.14.refs_2_), channel_id=1, source_target_pairs={{0,4},{4,0},{8,12},{12,8},{16,20},{20,16},{24,28},{28,24},{1,5},{5... | collective-permute-start | bytes 393224 | tf_op jit(solution)/shard_map/cond/branch_1_fun/ppermute | solution.py:558
  28.7 8.6 %collective-permute-start.18 = (bf16[2,128,128]{2,1,0:T(8,128)(2,1)S(1)}, bf16[2,128,128]{2,1,0:T(8,128)(2,1)S(1)}, u32[]{:S(2)}, u32[]{:S(2)}) collective-permute-start(bf16[2,128,128]{2,1,0:T(8,128)(2,1)S(1)} %get-tuple-element.59), channel_id=1, source_target_pairs={{0,0},{1,8},{2,16},{3,24},{4,4},{5,12},{6,20},{7,28},{8,1},{9,9},{... | collective-permute-start | bytes 196616 | tf_op jit(solution)/shard_map/cond/branch_1_fun/ppermute | solution.py:603
  37.3 1.3 %collective-permute-start.19 = (bf16[2,128,128]{2,1,0:T(8,128)(2,1)S(1)}, bf16[2,128,128]{2,1,0:T(8,128)(2,1)S(1)}, u32[]{:S(2)}, u32[]{:S(2)}) collective-permute-start(bf16[2,128,128]{2,1,0:T(8,128)(2,1)S(1)} %collective-permute-done.18.refs_0_), channel_id=1, source_target_pairs={{0,4},{4,0},{8,12},{12,8},{16,20},{20,16},{24,28},{28,24},{1,5},{5... | collective-permute-start | bytes 196616 | tf_op jit(solution)/shard_map/cond/branch_1_fun/ppermute | solution.py:604
  38.8 0.7 %copy-start = (f32[1,2,128,128]{3,2,1,0:T(8,128)}, f32[1,2,128,128]{3,2,1,0:T(8,128)S(1)}, u32[]{:S(2)}) copy-start(f32[1,2,128,128]{3,2,1,0:T(8,128)S(1)} %get-tuple-element.107) | copy-start | bytes 393220
where the time goes:
time: 39.6 us; the launch traced here: 39.5 us
  Pallas kernels  20.6 us (52%)
  waiting for transfers between devices  8.3 us (21%)
  starting transfers between devices  8.26 us (21%)
  between operations  1.33 us (3%)
  local copies, waits for them, and re-layouts  0.66 us (2%)
    pallas_call x1, Pallas kernels, start_compact(): pl.pallas_call(sort_kernel, out_shape=(jax.ShapeDtypeStruct((count, BLOCK...  12.1 us
    pallas_call x1, Pallas kernels, end_compact(): pl.pallas_call(functools.partial(product_kernel, len(mine)), out_shape=(j...  6.89 us
    ppermute x1, waiting for transfers between devices, finish(): first = lax.ppermute(sends, ('ia', 'ja'), moves(0))  6.02 us
    ppermute x3, starting transfers between devices, start_compact(): lax.ppermute(piece, 'ja', [(j, j ^ s) for j in range(columns_of_mesh)])  3.67 us
    ppermute x1, starting transfers between devices, finish(): first = lax.ppermute(sends, ('ia', 'ja'), moves(0))  2.58 us
    ppermute x3, starting transfers between devices, end_compact(): lax.ppermute(p, 'ia', [(i, i ^ 1) for i in range(rows_of_mesh)])  2 us
    pallas_call x1, Pallas kernels, first_piece(): pl.pallas_call(compact_kernel, out_shape=(jax.ShapeDtypeStruct((count, BL...  1.58 us
    ppermute x1, waiting for transfers between devices, finish(): lax.ppermute(first, 'ia', [(i, i ^ 1) for i in range(rows_of_mesh)])  1.25 us
  transfers between devices with their start and end apart: 8, of which 5 were waited for; matrix products, arithmetic and copies ran while one was open for 0% of the time, Pallas kernels for 31%

commit v1 on v0

--- a/solution.py
+++ b/solution.py
@@ -208,12 +208,41 @@
                 own_ref[aux, q, chunk * TILE : (chunk + 1) * TILE, :] = block[
                     chunk * TILE : (chunk + 1) * TILE, q * 128 : (q + 1) * 128
                 ]
+    sort_units(
+        [(0, 1)] * (pairs - 1) + [(0,)], lambda pair: moves[pair].wait(),
+        vir_ref, occ_ref, stage_ref, lists_ref, numbers, out_ref,
+    )
+
+
+def last_kernel(vir_ref, occ_ref, after_ref, stage_ref, tile_ref, out_ref, lists_ref):
+    del after_ref, tile_ref
+    places, numbers = places_of(vir_ref)
+    for label in range(2):
+        for place in range(SLOTS):
+            lists_ref[label, place] = -1
+    for tile, (label, place) in enumerate(places):
+        lists_ref[label, place] = tile
+    pairs = stage_ref.shape[0]
+    sort_units(
+        [()] * (pairs - 1) + [(1,)], lambda pair: None,
+        vir_ref, occ_ref, stage_ref, lists_ref, numbers, out_ref,
+    )
+
+
+def sort_units(chosen, ready, vir_ref, occ_ref, stage_ref, lists_ref, numbers, out_ref):
+    pairs, _, columns = stage_ref.shape
+    tiles = vir_ref.shape[0]
+    row = lax.axis_index("ia")
+    column = lax.axis_index("ja") * pairs
+    full = columns // 128
     lower = lax.broadcasted_iota(jnp.int32, (TILE, 128), 1) < TILE
     for pair in range(pairs):
-        moves[pair].wait()
+        if not chosen[pair]:
+            continue
+        ready(pair)
         symbol = occ_ref[row] ^ occ_ref[column + pair]
 
-        for label in range(2):
+        for label in chosen[pair]:
             rows_of = jnp.where(label == 1, numbers[1], numbers[0])
             columns_of = jnp.where((label ^ symbol) == 1, numbers[1], numbers[0])
 
@@ -258,9 +287,10 @@
             end = jnp.where(last == 1, numbers[1], numbers[0]) - 1
             label = last ^ symbol
             q = jnp.minimum(end // 2, BLOCKS - 1)
+            here = label == chosen[pair][0] if len(chosen[pair]) == 1 else label >= 0
             for upper in range(2):
 
-                @pl.when((lax.rem(end, 2) == upper) & (end < SLOTS))
+                @pl.when((lax.rem(end, 2) == upper) & (end < SLOTS) & here)
                 def _(upper=upper):
                     for place in range(SLOTS):
                         rows = tile_rows(jnp.maximum(lists_ref[label, place], 0))
@@ -269,7 +299,7 @@
                         both = [value, empty] if upper == 0 else [out_ref[at][:, :TILE], value]
                         out_ref[at] = jnp.concatenate(both, axis=1)
 
-        for label in range(2):
+        for label in chosen[pair]:
             number = jnp.where((label ^ symbol) == 1, numbers[1], numbers[0])
 
             def clear_block(q, carry):
@@ -286,7 +316,7 @@
                     value = out_ref[2 * pair + label, q, rows, :]
                     out_ref[2 * pair + label, q, rows, :] = jnp.concatenate([value[:, :TILE], empty], axis=1)
 
-        for label in range(2):
+        for label in chosen[pair]:
 
             def clear(place, carry):
                 for q in range(BLOCKS):
@@ -556,6 +586,21 @@
         total = count * columns_of_mesh
         rows = (total * window // BLOCK + 1) * BLOCK
         theirs = [lax.ppermute(p, "ia", [(i, i ^ 1) for i in range(rows_of_mesh)]) for p in mine]
+        tile = pl.pallas_call(
+            last_kernel,
+            out_shape=pltpu.VMEM(tile.shape, BF16),
+            in_specs=[smem, smem, pl.BlockSpec(memory_space=pl.ANY), vmem, pl.BlockSpec(memory_space=pl.ANY)],
+            out_specs=vmem,
+            input_output_aliases={4: 0},
+            scratch_shapes=[pltpu.SMEM((2, vir_irrep.shape[0]), jnp.int32)],
+            compiler_params=params(),
+            name="sort_last",
+        )(
+            vir_irrep, occ_irrep, mine[-1],
+            pltpu.with_memory_space_constraint(stage, pltpu.VMEM),
+            pltpu.with_memory_space_constraint(tile, pltpu.VMEM),
+        )
+        theirs, own, tile = lax.optimization_barrier((theirs, own, tile))
         return pl.pallas_call(
             functools.partial(product_kernel, len(mine)),
             out_shape=(

time: 39.6 us -> 38.9 us (0.982)
  waiting for transfers between devices: 8.3 us -> 4.74 us
  starting transfers between devices: 8.26 us -> 11.8 us
  Pallas kernels: 20.6 us -> 20 us
    ppermute x1, starting transfers between devices: 2.58 us -> 5.22 us  [finish(): first = lax.ppermute(sends, ('ia', 'ja'), moves(0))]
    ppermute x1, waiting for transfers between devices: 6.02 us -> 3.82 us  [finish(): first = lax.ppermute(sends, ('ia', 'ja'), moves(0))]
    pallas_call x0 -> x1, Pallas kernels: none -> 2.18 us  [end_compact(): pl.pallas_call(last_kernel, out_shape=pltpu.VMEM(tile.shape, BF16), in_sp...]
    pallas_call x1, Pallas kernels: 6.89 us -> 5.46 us  [end_compact(): pl.pallas_call(functools.partial(product_kernel, len(mine)), out_shape=(j...]
    pallas_call x1, Pallas kernels: 12.1 us -> 10.7 us  [start_compact(): pl.pallas_call(sort_kernel, out_shape=(jax.ShapeDtypeStruct((count, BLOCK...]
    ppermute x3, waiting for transfers between devices: 1.02 us -> 0.01 us  [end_compact(): lax.ppermute(p, 'ia', [(i, i ^ 1) for i in range(rows_of_mesh)])]
    ppermute x1, starting transfers between devices: 0.01 us -> 0.95 us  [finish(): lax.ppermute(first, 'ia', [(i, i ^ 1) for i in range(rows_of_mesh)])]
  transfers between devices with their start and end apart: 8 -> 8, of which waited for: 5 -> 2; matrix products, arithmetic and copies ran while one was open for 0% -> 0% of each run, Pallas kernels for 31% -> 33%
where the time goes in v1:
time: 38.9 us; the launch traced here: 38.8 us
  Pallas kernels  20 us (51%)
  starting transfers between devices  11.8 us (30%)
  waiting for transfers between devices  4.74 us (12%)
  between operations  1.33 us (3%)
  local copies, waits for them, and re-layouts  0.66 us (2%)
    pallas_call x1, Pallas kernels, start_compact(): pl.pallas_call(sort_kernel, out_shape=(jax.ShapeDtypeStruct((count, BLOCK...  10.7 us
    pallas_call x1, Pallas kernels, end_compact(): pl.pallas_call(functools.partial(product_kernel, len(mine)), out_shape=(j...  5.46 us
    ppermute x1, starting transfers between devices, finish(): first = lax.ppermute(sends, ('ia', 'ja'), moves(0))  5.22 us
    ppermute x1, waiting for transfers between devices, finish(): first = lax.ppermute(sends, ('ia', 'ja'), moves(0))  3.82 us
    ppermute x3, starting transfers between devices, start_compact(): lax.ppermute(piece, 'ja', [(j, j ^ s) for j in range(columns_of_mesh)])  3.67 us
    pallas_call x1, Pallas kernels, end_compact(): pl.pallas_call(last_kernel, out_shape=pltpu.VMEM(tile.shape, BF16), in_sp...  2.18 us
    ppermute x3, starting transfers between devices, end_compact(): lax.ppermute(p, 'ia', [(i, i ^ 1) for i in range(rows_of_mesh)])  1.96 us
    pallas_call x1, Pallas kernels, first_piece(): pl.pallas_call(compact_kernel, out_shape=(jax.ShapeDtypeStruct((count, BL...  1.58 us
  transfers between devices with their start and end apart: 8, of which 2 were waited for; matrix products, arithmetic and copies ran while one was open for 0% of the time, Pallas kernels for 33%

profile of v1, /device:TPU:7, one launch (start us, length us, event | category | flops | bytes accessed | tf_op | source)
XLA Modules:
  0.0 38.8 jit_solution(6677188217669184223)
XLA Ops:
  0.7 1.6 %compact_piece.1 = (bf16[1,8,64,128]{3,2,1,0:T(8,128)(2,1)S(1)}, s32[1]{0:T(128)}) custom-call(s32[25]{0:T(128)} %vir_hbm.1, s32[1]{0:T(128)S(6)} %copy.12.aux_ref, bf16[1,1600,128]{2,1,0:T(8,128)(2,1)} %bitcast.4), custom_call_target="tpu_custom_call" | custom-call | tf_op jit(solution)/shard_map/compact_piece/pallas_call | solution.py:529
  2.9 35.3 %conditional.1 = (f32[1,2,128,128]{3,2,1,0:T(8,128)S(1)}) conditional(s32[]{:T(128)} %bitcast.3, (bf16[1,128,1600]{1,2,0:T(8,128)(2,1)}, s32[25]{0:T(128)}, s32[1]{0:T(128)}, bf16[1,2,1600,1600]{3,2,1,0:T(8,128)(2,1)}, s32[8]{0:T(128)}) %tuple.14, (bf16[1,8,64,128]{3,2,1,0:T(8,128)(2,1)S(1)}, bf16[1,128,1600]{1,2,0:T(8,128)(2,1)}, s32[25]{0:T(128)}, ...), branch_computations={%region_0.0_spmd, %region_1.0_spmd} | conditional | flops 5242880000 | bytes 16909360 | solution.py:675
  2.9 0.0 copy-start.2
  2.9 0.0 copy-start.4
  2.9 1.4 %collective-permute-start.14 = (bf16[1,8,64,128]{3,2,1,0:T(8,128)(2,1)S(1)}, bf16[1,8,64,128]{3,2,1,0:T(8,128)(2,1)S(1)}, u32[]{:S(2)}, u32[]{:S(2)}) collective-permute-start(bf16[1,8,64,128]{3,2,1,0:T(8,128)(2,1)S(1)} %get-tuple-element.48.after_ref), channel_id=1, source_target_pairs={{0,1},{1,0},{2,3},{3,2},{4,5},{5,4},{6,7},{7,6},{8,9},{9,8},{10,11... | collective-permute-start | bytes 393224 | tf_op jit(solution)/shard_map/cond/branch_1_fun/ppermute | solution.py:554
  4.3 2.3 %collective-permute-start.13 = (bf16[1,8,64,128]{3,2,1,0:T(8,128)(2,1)S(1)}, bf16[1,8,64,128]{3,2,1,0:T(8,128)(2,1)S(1)}, u32[]{:S(2)}, u32[]{:S(2)}) collective-permute-start(bf16[1,8,64,128]{3,2,1,0:T(8,128)(2,1)S(1)} %get-tuple-element.48.after_ref), channel_id=1, source_target_pairs={{0,2},{1,3},{2,0},{3,1},{4,6},{5,7},{6,4},{7,5},{8,10},{9,11},{10,... | collective-permute-start | bytes 393224 | tf_op jit(solution)/shard_map/cond/branch_1_fun/ppermute | solution.py:554
  6.6 0.0 collective-permute-start.12
  6.6 10.7 %sort_amplitudes.1 = (bf16[1,8,128,128]{3,2,1,0:T(8,128)(2,1)S(1)}, bf16[4,8,1024,128]{3,2,1,0:T(8,128)(2,1)S(1)}, bf16[2,1600,1600]{2,1,0:T(8,128)(2,1)S(1)}) custom-call(s32[25]{0:T(128)} %get-tuple-element.45.vir_ref, s32[8]{0:T(128)} %get-tuple-element.46.occ_ref, s32[1]{0:T(128)} %get-tuple-element.47.aux_ref, ...), custom_call_target="tpu_custom_call" | custom-call | flops 33554432 | bytes 10240000 | tf_op jit(solution)/shard_map/cond/branch_1_fun/sort_amplitudes/pallas_call | solution.py:557
  17.4 0.0 collective-permute-done.14.after_ref.refs_2_
  17.4 0.0 collective-permute-done.13.refs_1_
  17.4 0.0 collective-permute-done.12.refs_0_
  17.4 1.4 %collective-permute-start.15 = (bf16[1,8,64,128]{3,2,1,0:T(8,128)(2,1)S(1)}, bf16[1,8,64,128]{3,2,1,0:T(8,128)(2,1)S(1)}, u32[]{:S(2)}, u32[]{:S(2)}) collective-permute-start(bf16[1,8,64,128]{3,2,1,0:T(8,128)(2,1)S(1)} %collective-permute-done.12.refs_0_), channel_id=1, source_target_pairs={{0,4},{4,0},{8,12},{12,8},{16,20},{20,16},{24,28},{28,24},{1,5},{5... | collective-permute-start | bytes 393224 | tf_op jit(solution)/shard_map/cond/branch_1_fun/ppermute | solution.py:588
  18.8 0.1 collective-permute-start.16
  18.9 0.4 %collective-permute-start.17 = (bf16[1,8,64,128]{3,2,1,0:T(8,128)(2,1)S(1)}, bf16[1,8,64,128]{3,2,1,0:T(8,128)(2,1)S(1)}, u32[]{:S(2)}, u32[]{:S(2)}) collective-permute-start(bf16[1,8,64,128]{3,2,1,0:T(8,128)(2,1)S(1)} %collective-permute-done.14.after_ref.refs_2_), channel_id=1, source_target_pairs={{0,4},{4,0},{8,12},{12,8},{16,20},{20,16},{24,28},{28,24},{1,5},{5... | collective-permute-start | bytes 393224 | tf_op jit(solution)/shard_map/cond/branch_1_fun/ppermute | solution.py:588
  19.3 0.0 copy-done.2
  19.4 0.0 copy-done.4
  19.4 2.2 %sort_last.1.sorted_ref = bf16[4,8,1024,128]{3,2,1,0:T(8,128)(2,1)S(1)} custom-call(s32[25]{0:T(128)S(1)} %copy-done.2, s32[8]{0:T(128)S(1)} %copy-done.4, bf16[1,8,64,128]{3,2,1,0:T(8,128)(2,1)S(1)} %collective-permute-done.14.after_ref.refs_2_, bf16[2,1600,1600]{2,1,0:T(8,128)(2,1)S(1)} %get-tuple-element.56.stage_ref, ...), custom_call_target="tpu_custom_call", output_to_operand_aliasing={{}: (4, {})} | custom-call | tf_op jit(solution)/shard_map/cond/branch_1_fun/sort_last/pallas_call | solution.py:589
  21.5 0.0 collective-permute-done.15.refs_3_
  21.5 0.0 collective-permute-done.16.refs_4_
  21.6 0.0 collective-permute-done.17.refs_5_
  21.6 5.5 %products.1 = (f32[2,128,128]{2,1,0:T(8,128)S(1)}, bf16[2,128,128]{2,1,0:T(8,128)(2,1)S(1)}) custom-call(s32[25]{0:T(128)S(1)} %copy-done.2, s32[8]{0:T(128)S(1)} %copy-done.4, s32[1]{0:T(128)} %get-tuple-element.47.aux_ref, bf16[1,8,128,128]{3,2,1,0:T(8,128)(2,1)S(1)} %get-tuple-element.58.own_ref, bf16[4,8,1024,128]{3,2,1,0:T(8,128)(2,1)S(1)} %sort_last.1.sorted_ref, ...), custom_call_target="tpu_custom_call" | custom-call | flops 2147483648 | bytes 1048576 | tf_op jit(solution)/shard_map/cond/branch_1_fun/products/pallas_call | solution.py:604
  27.0 5.2 %collective-permute-start.18 = (bf16[2,128,128]{2,1,0:T(8,128)(2,1)S(1)}, bf16[2,128,128]{2,1,0:T(8,128)(2,1)S(1)}, u32[]{:S(2)}, u32[]{:S(2)}) collective-permute-start(bf16[2,128,128]{2,1,0:T(8,128)(2,1)S(1)} %get-tuple-element.64), channel_id=1, source_target_pairs={{0,0},{1,8},{2,16},{3,24},{4,4},{5,12},{6,20},{7,28},{8,1},{9,9},{... | collective-permute-start | bytes 196616 | tf_op jit(solution)/shard_map/cond/branch_1_fun/ppermute | solution.py:648
  32.3 3.8 %collective-permute-done.18.refs_0_ = bf16[2,128,128]{2,1,0:T(8,128)(2,1)S(1)} collective-permute-done((bf16[2,128,128]{2,1,0:T(8,128)(2,1)S(1)}, bf16[2,128,128]{2,1,0:T(8,128)(2,1)S(1)}, u32[]{:S(2)}, u32[]{:S(2)}) %collective-permute-start.18) | collective-permute-done | bytes 65568 | tf_op jit(solution)/shard_map/cond/branch_1_fun/ppermute | solution.py:648
  36.1 0.9 %collective-permute-start.19 = (bf16[2,128,128]{2,1,0:T(8,128)(2,1)S(1)}, bf16[2,128,128]{2,1,0:T(8,128)(2,1)S(1)}, u32[]{:S(2)}, u32[]{:S(2)}) collective-permute-start(bf16[2,128,128]{2,1,0:T(8,128)(2,1)S(1)} %collective-permute-done.18.refs_0_), channel_id=1, source_target_pairs={{0,4},{4,0},{8,12},{12,8},{16,20},{20,16},{24,28},{28,24},{1,5},{5... | collective-permute-start | bytes 196616 | tf_op jit(solution)/shard_map/cond/branch_1_fun/ppermute | solution.py:649
  37.0 0.9 %collective-permute-done.19.refs_1_ = bf16[2,128,128]{2,1,0:T(8,128)(2,1)S(1)} collective-permute-done((bf16[2,128,128]{2,1,0:T(8,128)(2,1)S(1)}, bf16[2,128,128]{2,1,0:T(8,128)(2,1)S(1)}, u32[]{:S(2)}, u32[]{:S(2)}) %collective-permute-start.19) | collective-permute-done | bytes 65568 | tf_op jit(solution)/shard_map/cond/branch_1_fun/ppermute | solution.py:649
  38.2 0.0 copy-start
  38.2 0.6 %copy-done = f32[1,2,128,128]{3,2,1,0:T(8,128)} copy-done((f32[1,2,128,128]{3,2,1,0:T(8,128)}, f32[1,2,128,128]{3,2,1,0:T(8,128)S(1)}, u32[]{:S(2)}) %copy-start) | copy-done | bytes 131096
  (1 shorter events, 0.0 us)
Async XLA Ops:
  2.9 16.4 %copy-start.2 = (s32[25]{0:T(128)S(1)}, s32[25]{0:T(128)}, u32[]{:S(2)}) copy-start(s32[25]{0:T(128)} %get-tuple-element.45.vir_ref) | copy-start | bytes 304 | tf_op jit(solution)/shard_map/cond
  2.9 16.4 %copy-start.4 = (s32[8]{0:T(128)S(1)}, s32[8]{0:T(128)}, u32[]{:S(2)}) copy-start(s32[8]{0:T(128)} %get-tuple-element.46.occ_ref) | copy-start | bytes 100 | tf_op jit(solution)/shard_map/cond
  2.9 14.4 %collective-permute-start.14 = (bf16[1,8,64,128]{3,2,1,0:T(8,128)(2,1)S(1)}, bf16[1,8,64,128]{3,2,1,0:T(8,128)(2,1)S(1)}, u32[]{:S(2)}, u32[]{:S(2)}) collective-permute-start(bf16[1,8,64,128]{3,2,1,0:T(8,128)(2,1)S(1)} %get-tuple-element.48.after_ref), channel_id=1, source_target_pairs={{0,1},{1,0},{2,3},{3,2},{4,5},{5,4},{6,7},{7,6},{8,9},{9,8},{10,11... | collective-permute-start | bytes 393224 | tf_op jit(solution)/shard_map/cond/branch_1_fun/ppermute | solution.py:554
  4.3 13.1 %collective-permute-start.13 = (bf16[1,8,64,128]{3,2,1,0:T(8,128)(2,1)S(1)}, bf16[1,8,64,128]{3,2,1,0:T(8,128)(2,1)S(1)}, u32[]{:S(2)}, u32[]{:S(2)}) collective-permute-start(bf16[1,8,64,128]{3,2,1,0:T(8,128)(2,1)S(1)} %get-tuple-element.48.after_ref), channel_id=1, source_target_pairs={{0,2},{1,3},{2,0},{3,1},{4,6},{5,7},{6,4},{7,5},{8,10},{9,11},{10,... | collective-permute-start | bytes 393224 | tf_op jit(solution)/shard_map/cond/branch_1_fun/ppermute | solution.py:554
  6.6 10.8 %collective-permute-start.12 = (bf16[1,8,64,128]{3,2,1,0:T(8,128)(2,1)S(1)}, bf16[1,8,64,128]{3,2,1,0:T(8,128)(2,1)S(1)}, u32[]{:S(2)}, u32[]{:S(2)}) collective-permute-start(bf16[1,8,64,128]{3,2,1,0:T(8,128)(2,1)S(1)} %get-tuple-element.48.after_ref), channel_id=1, source_target_pairs={{0,3},{1,2},{2,1},{3,0},{4,7},{5,6},{6,5},{7,4},{8,11},{9,10},{10,... | collective-permute-start | bytes 393224 | tf_op jit(solution)/shard_map/cond/branch_1_fun/ppermute | solution.py:554
  17.4 4.2 %collective-permute-start.15 = (bf16[1,8,64,128]{3,2,1,0:T(8,128)(2,1)S(1)}, bf16[1,8,64,128]{3,2,1,0:T(8,128)(2,1)S(1)}, u32[]{:S(2)}, u32[]{:S(2)}) collective-permute-start(bf16[1,8,64,128]{3,2,1,0:T(8,128)(2,1)S(1)} %collective-permute-done.12.refs_0_), channel_id=1, source_target_pairs={{0,4},{4,0},{8,12},{12,8},{16,20},{20,16},{24,28},{28,24},{1,5},{5... | collective-permute-start | bytes 393224 | tf_op jit(solution)/shard_map/cond/branch_1_fun/ppermute | solution.py:588
  18.8 2.7 %collective-permute-start.16 = (bf16[1,8,64,128]{3,2,1,0:T(8,128)(2,1)S(1)}, bf16[1,8,64,128]{3,2,1,0:T(8,128)(2,1)S(1)}, u32[]{:S(2)}, u32[]{:S(2)}) collective-permute-start(bf16[1,8,64,128]{3,2,1,0:T(8,128)(2,1)S(1)} %collective-permute-done.13.refs_1_), channel_id=1, source_target_pairs={{0,4},{4,0},{8,12},{12,8},{16,20},{20,16},{24,28},{28,24},{1,5},{5... | collective-permute-start | bytes 393224 | tf_op jit(solution)/shard_map/cond/branch_1_fun/ppermute | solution.py:588
  18.9 2.6 %collective-permute-start.17 = (bf16[1,8,64,128]{3,2,1,0:T(8,128)(2,1)S(1)}, bf16[1,8,64,128]{3,2,1,0:T(8,128)(2,1)S(1)}, u32[]{:S(2)}, u32[]{:S(2)}) collective-permute-start(bf16[1,8,64,128]{3,2,1,0:T(8,128)(2,1)S(1)} %collective-permute-done.14.after_ref.refs_2_), channel_id=1, source_target_pairs={{0,4},{4,0},{8,12},{12,8},{16,20},{20,16},{24,28},{28,24},{1,5},{5... | collective-permute-start | bytes 393224 | tf_op jit(solution)/shard_map/cond/branch_1_fun/ppermute | solution.py:588
  27.0 9.0 %collective-permute-start.18 = (bf16[2,128,128]{2,1,0:T(8,128)(2,1)S(1)}, bf16[2,128,128]{2,1,0:T(8,128)(2,1)S(1)}, u32[]{:S(2)}, u32[]{:S(2)}) collective-permute-start(bf16[2,128,128]{2,1,0:T(8,128)(2,1)S(1)} %get-tuple-element.64), channel_id=1, source_target_pairs={{0,0},{1,8},{2,16},{3,24},{4,4},{5,12},{6,20},{7,28},{8,1},{9,9},{... | collective-permute-start | bytes 196616 | tf_op jit(solution)/shard_map/cond/branch_1_fun/ppermute | solution.py:648
  36.1 1.9 %collective-permute-start.19 = (bf16[2,128,128]{2,1,0:T(8,128)(2,1)S(1)}, bf16[2,128,128]{2,1,0:T(8,128)(2,1)S(1)}, u32[]{:S(2)}, u32[]{:S(2)}) collective-permute-start(bf16[2,128,128]{2,1,0:T(8,128)(2,1)S(1)} %collective-permute-done.18.refs_0_), channel_id=1, source_target_pairs={{0,4},{4,0},{8,12},{12,8},{16,20},{20,16},{24,28},{28,24},{1,5},{5... | collective-permute-start | bytes 196616 | tf_op jit(solution)/shard_map/cond/branch_1_fun/ppermute | solution.py:649
  38.2 0.7 %copy-start = (f32[1,2,128,128]{3,2,1,0:T(8,128)}, f32[1,2,128,128]{3,2,1,0:T(8,128)S(1)}, u32[]{:S(2)}) copy-start(f32[1,2,128,128]{3,2,1,0:T(8,128)S(1)} %get-tuple-element.112) | copy-start | bytes 393220
